TPU v7x, 1024 devices: a whole 4x4x32 slice. The times are simulated.
1024 devices in a mesh: row: 16 (over z_lo, core), col: 16 (over y, x), layer: 4 (over z_hi).
Axes of the slice: x: 4, y: 4, z: 32 (z_hi: 4, z_lo: 8; z = z_hi * 8 + z_lo), core: 2. Of those that a mesh axis runs over, the one named last changes fastest.
Arguments:
- dens_blocks: bfloat16 [16, 16, 4, 16, 64, 128], P('row', 'col', 'layer'), may hold values from -0.0625 to 0.0625
- dens_ids: int32 [16, 16, 4, 16, 2], P('row', 'col', 'layer'), may hold values from 0 to 3, as said below
- ham_blocks: bfloat16 [16, 16, 4, 4, 64, 64], P('row', 'col', 'layer'), may hold values from -6 to 6
- ham_ids: int32 [16, 16, 4, 4, 1], P('row', 'col', 'layer'), may hold values from 0 to 1, as said below
- ovl_blocks: bfloat16 [16, 16, 4, 4, 64, 64], P('row', 'col', 'layer'), may hold values from -6 to 6
- ovl_ids: int32 [16, 16, 4, 4, 1], P('row', 'col', 'layer'), may hold values from 0 to 1, as said below
Outputs:
- dens_ham: float32 [256, 64, 2048], P(('row', 'layer'), None, 'col')
- dens_ovl: float32 [256, 64, 2048], P(('row', 'layer'), None, 'col')
Inputs may be any that keep to these rules, and one draw needn't show every extreme that they name: `dens_ids`: the 2 ids of one block row of a density tile are distinct. `ham_ids`: the 1 ids of one block row of a Hamiltonian tile are distinct. `ovl_ids`: the 1 ids of one block row of a tile of S are distinct.
All inputs are finite; a program needn't handle non-finite values.
Results may differ from a plain program's by a relative error of at most 0.0003.
Values may be sent and summed in bfloat16 or wider, within the bound.
A program may use at most 32 MiB of HBM per device.

v0:
```python
import jax
import jax.numpy as jnp
from jax import lax
from jax.sharding import PartitionSpec as P

CB = 2


def passed_along(block, axis, distance):
    devices = range(lax.axis_size(axis))
    route = [((i - distance) % len(devices), i) for i in devices]
    return lax.ppermute(block, axis, route)


def densify(tile_vals, tile_ids, columns):
    onehot = (tile_ids[:, :, None] == jnp.arange(columns, dtype=jnp.int32)[None, None, :]).astype(
        jnp.bfloat16
    )
    blocks = tile_vals.reshape(
        tile_vals.shape[0], tile_vals.shape[1], tile_ids.shape[1], tile_vals.shape[1]
    )
    dense_tile = jnp.einsum("kxbw,kbc->kxcw", blocks, onehot, preferred_element_type=jnp.float32)
    return dense_tile.reshape(
        tile_vals.shape[0], tile_vals.shape[1], columns * tile_vals.shape[1]
    ).astype(jnp.bfloat16)


def product(dens_tile, dens_index, ham_tile, ham_index, ovl_tile, ovl_index):
    stacked = jnp.stack([densify(ham_tile, ham_index, CB), densify(ovl_tile, ovl_index, CB)])
    selected = jnp.take(stacked, dens_index, axis=1)
    selected = selected.reshape(
        2, dens_index.shape[0], dens_index.shape[1] * stacked.shape[2], stacked.shape[3]
    )
    return jnp.einsum("rxk,mrkw->mrxw", dens_tile, selected, preferred_element_type=jnp.float32)


def local(dens_blocks, dens_ids, ham_blocks, ham_ids, ovl_blocks, ovl_ids):
    grid_size = lax.axis_size("col")
    dens_tile = dens_blocks[0, 0, 0]
    dens_index = dens_ids[0, 0, 0]
    totals = jnp.zeros(
        (2, dens_tile.shape[0], dens_tile.shape[1], CB * dens_tile.shape[1]), jnp.float32
    )

    def advance(turn_index, carry):
        d_vals, d_ids, h_vals, h_ids, o_vals, o_ids, running = carry
        running = running + product(d_vals, d_ids, h_vals, h_ids, o_vals, o_ids)
        d_vals, d_ids = passed_along((d_vals, d_ids), "col", -1)
        h_vals, h_ids, o_vals, o_ids = passed_along((h_vals, h_ids, o_vals, o_ids), "row", -1)
        return (d_vals, d_ids, h_vals, h_ids, o_vals, o_ids, running)

    start_carry = (
        dens_tile,
        dens_index,
        ham_blocks[0, 0, 0],
        ham_ids[0, 0, 0],
        ovl_blocks[0, 0, 0],
        ovl_ids[0, 0, 0],
        totals,
    )
    final = lax.fori_loop(0, grid_size - 1, advance, start_carry)
    totals = final[6] + product(final[0], final[1], final[2], final[3], final[4], final[5])
    summed = lax.psum_scatter(totals, "layer", scatter_dimension=1, tiled=True)
    return (summed[0], summed[1])


def solution(mesh):
    placed = (
        P("row", "col", "layer", None, None, None),
        P("row", "col", "layer", None, None),
        P("row", "col", "layer", None, None, None),
        P("row", "col", "layer", None, None),
        P("row", "col", "layer", None, None, None),
        P("row", "col", "layer", None, None),
    )
    return jax.shard_map(
        local,
        mesh=mesh,
        in_specs=placed,
        out_specs=(P(("row", "layer"), None, "col"), P(("row", "layer"), None, "col")),
        check_vma=False,
    )
```

profile of v0, /device:TPU:1, one launch (start us, length us, event | category | flops | bytes accessed | tf_op | source)
XLA Modules:
  0.0 625.8 jit_solution(4547531660838583454)
XLA Ops:
  8.8 493.5 %while.23 = (s32[]{:T(128)}, bf16[16,64,128]{2,1,0:T(8,128)(2,1)S(1)}, s32[16,2]{1,0:T(8,128)S(1)}, bf16[4,64,64]{2,1,0:T(8,128)(2,1)S(1)}, s32[4,1]{0,1:T(1,128...) while((s32[]{:T(128)}, ...), condition=%wide.region_1.3_spmd.clone, body=%wide.region_0.2_spmd.clone.sunk | while | flops 68388160 | bytes 12654975 | solution.py:61
  8.8 7.7 %collective-permute-start.1 = (s32[16,2]{1,0:T(8,128)S(1)}, s32[16,2]{1,0:T(8,128)S(1)}, u32[]{:S(2)}, u32[]{:S(2)}) collective-permute-start(s32[16,2]{1,0:T(8,128)S(1)} %copy.35), channel_id=1, source_target_pairs={{4,0},{8,4},{12,8},{16,12},{20,16},{24,20},{28,24},{32,28},{36,32}... | collective-permute-start | bytes 392 | tf_op jit(solution)/shard_map/while/body/eval_jaxpr/ppermute | solution.py:12
  18.9 9.8 %collective-permute-start.2 = (bf16[4,64,64]{2,1,0:T(8,128)(2,1)S(1)}, bf16[4,64,64]{2,1,0:T(8,128)(2,1)S(1)}, u32[]{:S(2)}, u32[]{:S(2)}) collective-permute-start(bf16[4,64,64]{2,1,0:T(8,128)(2,1)S(1)} %copy.36), channel_id=1, source_target_pairs={{64,0},{128,64},{192,128},{256,192},{320,256},{384,320},{448,384},... | collective-permute-start | bytes 98312 | tf_op jit(solution)/shard_map/while/body/eval_jaxpr/ppermute | solution.py:12
  28.7 5.4 collective-permute-start.4
  34.1 3.1 collective-permute-start.3
  41.6 2.9 collective-permute-done.5
  49.0 8.0 %collective-permute-start.2 = (bf16[4,64,64]{2,1,0:T(8,128)(2,1)S(1)}, bf16[4,64,64]{2,1,0:T(8,128)(2,1)S(1)}, u32[]{:S(2)}, u32[]{:S(2)}) collective-permute-start(bf16[4,64,64]{2,1,0:T(8,128)(2,1)S(1)} %copy.36), channel_id=1, source_target_pairs={{64,0},{128,64},{192,128},{256,192},{320,256},{384,320},{448,384},... | collective-permute-start | bytes 98312 | tf_op jit(solution)/shard_map/while/body/eval_jaxpr/ppermute | solution.py:12
  57.0 9.6 %collective-permute-start.4 = (bf16[4,64,64]{2,1,0:T(8,128)(2,1)S(1)}, bf16[4,64,64]{2,1,0:T(8,128)(2,1)S(1)}, u32[]{:S(2)}, u32[]{:S(2)}) collective-permute-start(bf16[4,64,64]{2,1,0:T(8,128)(2,1)S(1)} %copy.38), channel_id=1, source_target_pairs={{64,0},{128,64},{192,128},{256,192},{320,256},{384,320},{448,384},... | collective-permute-start | bytes 98312 | tf_op jit(solution)/shard_map/while/body/eval_jaxpr/ppermute | solution.py:12
  73.4 2.9 collective-permute-done.5
  76.4 4.6 collective-permute-start.1
  83.4 7.4 %collective-permute-start.2 = (bf16[4,64,64]{2,1,0:T(8,128)(2,1)S(1)}, bf16[4,64,64]{2,1,0:T(8,128)(2,1)S(1)}, u32[]{:S(2)}, u32[]{:S(2)}) collective-permute-start(bf16[4,64,64]{2,1,0:T(8,128)(2,1)S(1)} %copy.36), channel_id=1, source_target_pairs={{64,0},{128,64},{192,128},{256,192},{320,256},{384,320},{448,384},... | collective-permute-start | bytes 98312 | tf_op jit(solution)/shard_map/while/body/eval_jaxpr/ppermute | solution.py:12
  90.9 9.6 %collective-permute-start.4 = (bf16[4,64,64]{2,1,0:T(8,128)(2,1)S(1)}, bf16[4,64,64]{2,1,0:T(8,128)(2,1)S(1)}, u32[]{:S(2)}, u32[]{:S(2)}) collective-permute-start(bf16[4,64,64]{2,1,0:T(8,128)(2,1)S(1)} %copy.38), channel_id=1, source_target_pairs={{64,0},{128,64},{192,128},{256,192},{320,256},{384,320},{448,384},... | collective-permute-start | bytes 98312 | tf_op jit(solution)/shard_map/while/body/eval_jaxpr/ppermute | solution.py:12
  107.3 2.9 collective-permute-done.5
  114.7 7.4 %collective-permute-start.2 = (bf16[4,64,64]{2,1,0:T(8,128)(2,1)S(1)}, bf16[4,64,64]{2,1,0:T(8,128)(2,1)S(1)}, u32[]{:S(2)}, u32[]{:S(2)}) collective-permute-start(bf16[4,64,64]{2,1,0:T(8,128)(2,1)S(1)} %copy.36), channel_id=1, source_target_pairs={{64,0},{128,64},{192,128},{256,192},{320,256},{384,320},{448,384},... | collective-permute-start | bytes 98312 | tf_op jit(solution)/shard_map/while/body/eval_jaxpr/ppermute | solution.py:12
  122.1 9.6 %collective-permute-start.4 = (bf16[4,64,64]{2,1,0:T(8,128)(2,1)S(1)}, bf16[4,64,64]{2,1,0:T(8,128)(2,1)S(1)}, u32[]{:S(2)}, u32[]{:S(2)}) collective-permute-start(bf16[4,64,64]{2,1,0:T(8,128)(2,1)S(1)} %copy.38), channel_id=1, source_target_pairs={{64,0},{128,64},{192,128},{256,192},{320,256},{384,320},{448,384},... | collective-permute-start | bytes 98312 | tf_op jit(solution)/shard_map/while/body/eval_jaxpr/ppermute | solution.py:12
  138.5 2.9 collective-permute-done.5
  141.5 4.3 collective-permute-start.1
  148.3 7.4 %collective-permute-start.2 = (bf16[4,64,64]{2,1,0:T(8,128)(2,1)S(1)}, bf16[4,64,64]{2,1,0:T(8,128)(2,1)S(1)}, u32[]{:S(2)}, u32[]{:S(2)}) collective-permute-start(bf16[4,64,64]{2,1,0:T(8,128)(2,1)S(1)} %copy.36), channel_id=1, source_target_pairs={{64,0},{128,64},{192,128},{256,192},{320,256},{384,320},{448,384},... | collective-permute-start | bytes 98312 | tf_op jit(solution)/shard_map/while/body/eval_jaxpr/ppermute | solution.py:12
  155.7 9.6 %collective-permute-start.4 = (bf16[4,64,64]{2,1,0:T(8,128)(2,1)S(1)}, bf16[4,64,64]{2,1,0:T(8,128)(2,1)S(1)}, u32[]{:S(2)}, u32[]{:S(2)}) collective-permute-start(bf16[4,64,64]{2,1,0:T(8,128)(2,1)S(1)} %copy.38), channel_id=1, source_target_pairs={{64,0},{128,64},{192,128},{256,192},{320,256},{384,320},{448,384},... | collective-permute-start | bytes 98312 | tf_op jit(solution)/shard_map/while/body/eval_jaxpr/ppermute | solution.py:12
  179.5 7.4 %collective-permute-start.2 = (bf16[4,64,64]{2,1,0:T(8,128)(2,1)S(1)}, bf16[4,64,64]{2,1,0:T(8,128)(2,1)S(1)}, u32[]{:S(2)}, u32[]{:S(2)}) collective-permute-start(bf16[4,64,64]{2,1,0:T(8,128)(2,1)S(1)} %copy.36), channel_id=1, source_target_pairs={{64,0},{128,64},{192,128},{256,192},{320,256},{384,320},{448,384},... | collective-permute-start | bytes 98312 | tf_op jit(solution)/shard_map/while/body/eval_jaxpr/ppermute | solution.py:12
  187.0 9.6 %collective-permute-start.4 = (bf16[4,64,64]{2,1,0:T(8,128)(2,1)S(1)}, bf16[4,64,64]{2,1,0:T(8,128)(2,1)S(1)}, u32[]{:S(2)}, u32[]{:S(2)}) collective-permute-start(bf16[4,64,64]{2,1,0:T(8,128)(2,1)S(1)} %copy.38), channel_id=1, source_target_pairs={{64,0},{128,64},{192,128},{256,192},{320,256},{384,320},{448,384},... | collective-permute-start | bytes 98312 | tf_op jit(solution)/shard_map/while/body/eval_jaxpr/ppermute | solution.py:12
  206.4 4.3 collective-permute-start.1
  213.1 7.4 %collective-permute-start.2 = (bf16[4,64,64]{2,1,0:T(8,128)(2,1)S(1)}, bf16[4,64,64]{2,1,0:T(8,128)(2,1)S(1)}, u32[]{:S(2)}, u32[]{:S(2)}) collective-permute-start(bf16[4,64,64]{2,1,0:T(8,128)(2,1)S(1)} %copy.36), channel_id=1, source_target_pairs={{64,0},{128,64},{192,128},{256,192},{320,256},{384,320},{448,384},... | collective-permute-start | bytes 98312 | tf_op jit(solution)/shard_map/while/body/eval_jaxpr/ppermute | solution.py:12
  220.6 9.6 %collective-permute-start.4 = (bf16[4,64,64]{2,1,0:T(8,128)(2,1)S(1)}, bf16[4,64,64]{2,1,0:T(8,128)(2,1)S(1)}, u32[]{:S(2)}, u32[]{:S(2)}) collective-permute-start(bf16[4,64,64]{2,1,0:T(8,128)(2,1)S(1)} %copy.38), channel_id=1, source_target_pairs={{64,0},{128,64},{192,128},{256,192},{320,256},{384,320},{448,384},... | collective-permute-start | bytes 98312 | tf_op jit(solution)/shard_map/while/body/eval_jaxpr/ppermute | solution.py:12
  237.0 2.9 collective-permute-done.5
  242.2 3.5 collective-permute-start
  245.7 7.4 %collective-permute-start.2 = (bf16[4,64,64]{2,1,0:T(8,128)(2,1)S(1)}, bf16[4,64,64]{2,1,0:T(8,128)(2,1)S(1)}, u32[]{:S(2)}, u32[]{:S(2)}) collective-permute-start(bf16[4,64,64]{2,1,0:T(8,128)(2,1)S(1)} %copy.36), channel_id=1, source_target_pairs={{64,0},{128,64},{192,128},{256,192},{320,256},{384,320},{448,384},... | collective-permute-start | bytes 98312 | tf_op jit(solution)/shard_map/while/body/eval_jaxpr/ppermute | solution.py:12
  253.1 9.6 %collective-permute-start.4 = (bf16[4,64,64]{2,1,0:T(8,128)(2,1)S(1)}, bf16[4,64,64]{2,1,0:T(8,128)(2,1)S(1)}, u32[]{:S(2)}, u32[]{:S(2)}) collective-permute-start(bf16[4,64,64]{2,1,0:T(8,128)(2,1)S(1)} %copy.38), channel_id=1, source_target_pairs={{64,0},{128,64},{192,128},{256,192},{320,256},{384,320},{448,384},... | collective-permute-start | bytes 98312 | tf_op jit(solution)/shard_map/while/body/eval_jaxpr/ppermute | solution.py:12
  269.5 2.9 collective-permute-done.5
  272.5 5.5 collective-permute-start.1
  280.6 7.4 %collective-permute-start.2 = (bf16[4,64,64]{2,1,0:T(8,128)(2,1)S(1)}, bf16[4,64,64]{2,1,0:T(8,128)(2,1)S(1)}, u32[]{:S(2)}, u32[]{:S(2)}) collective-permute-start(bf16[4,64,64]{2,1,0:T(8,128)(2,1)S(1)} %copy.36), channel_id=1, source_target_pairs={{64,0},{128,64},{192,128},{256,192},{320,256},{384,320},{448,384},... | collective-permute-start | bytes 98312 | tf_op jit(solution)/shard_map/while/body/eval_jaxpr/ppermute | solution.py:12
  288.0 9.6 %collective-permute-start.4 = (bf16[4,64,64]{2,1,0:T(8,128)(2,1)S(1)}, bf16[4,64,64]{2,1,0:T(8,128)(2,1)S(1)}, u32[]{:S(2)}, u32[]{:S(2)}) collective-permute-start(bf16[4,64,64]{2,1,0:T(8,128)(2,1)S(1)} %copy.38), channel_id=1, source_target_pairs={{64,0},{128,64},{192,128},{256,192},{320,256},{384,320},{448,384},... | collective-permute-start | bytes 98312 | tf_op jit(solution)/shard_map/while/body/eval_jaxpr/ppermute | solution.py:12
  311.8 7.4 %collective-permute-start.2 = (bf16[4,64,64]{2,1,0:T(8,128)(2,1)S(1)}, bf16[4,64,64]{2,1,0:T(8,128)(2,1)S(1)}, u32[]{:S(2)}, u32[]{:S(2)}) collective-permute-start(bf16[4,64,64]{2,1,0:T(8,128)(2,1)S(1)} %copy.36), channel_id=1, source_target_pairs={{64,0},{128,64},{192,128},{256,192},{320,256},{384,320},{448,384},... | collective-permute-start | bytes 98312 | tf_op jit(solution)/shard_map/while/body/eval_jaxpr/ppermute | solution.py:12
  319.2 9.6 %collective-permute-start.4 = (bf16[4,64,64]{2,1,0:T(8,128)(2,1)S(1)}, bf16[4,64,64]{2,1,0:T(8,128)(2,1)S(1)}, u32[]{:S(2)}, u32[]{:S(2)}) collective-permute-start(bf16[4,64,64]{2,1,0:T(8,128)(2,1)S(1)} %copy.38), channel_id=1, source_target_pairs={{64,0},{128,64},{192,128},{256,192},{320,256},{384,320},{448,384},... | collective-permute-start | bytes 98312 | tf_op jit(solution)/shard_map/while/body/eval_jaxpr/ppermute | solution.py:12
  338.6 4.6 collective-permute-start.1
  345.7 7.4 %collective-permute-start.2 = (bf16[4,64,64]{2,1,0:T(8,128)(2,1)S(1)}, bf16[4,64,64]{2,1,0:T(8,128)(2,1)S(1)}, u32[]{:S(2)}, u32[]{:S(2)}) collective-permute-start(bf16[4,64,64]{2,1,0:T(8,128)(2,1)S(1)} %copy.36), channel_id=1, source_target_pairs={{64,0},{128,64},{192,128},{256,192},{320,256},{384,320},{448,384},... | collective-permute-start | bytes 98312 | tf_op jit(solution)/shard_map/while/body/eval_jaxpr/ppermute | solution.py:12
  353.2 9.6 %collective-permute-start.4 = (bf16[4,64,64]{2,1,0:T(8,128)(2,1)S(1)}, bf16[4,64,64]{2,1,0:T(8,128)(2,1)S(1)}, u32[]{:S(2)}, u32[]{:S(2)}) collective-permute-start(bf16[4,64,64]{2,1,0:T(8,128)(2,1)S(1)} %copy.38), channel_id=1, source_target_pairs={{64,0},{128,64},{192,128},{256,192},{320,256},{384,320},{448,384},... | collective-permute-start | bytes 98312 | tf_op jit(solution)/shard_map/while/body/eval_jaxpr/ppermute | solution.py:12
  376.9 7.4 %collective-permute-start.2 = (bf16[4,64,64]{2,1,0:T(8,128)(2,1)S(1)}, bf16[4,64,64]{2,1,0:T(8,128)(2,1)S(1)}, u32[]{:S(2)}, u32[]{:S(2)}) collective-permute-start(bf16[4,64,64]{2,1,0:T(8,128)(2,1)S(1)} %copy.36), channel_id=1, source_target_pairs={{64,0},{128,64},{192,128},{256,192},{320,256},{384,320},{448,384},... | collective-permute-start | bytes 98312 | tf_op jit(solution)/shard_map/while/body/eval_jaxpr/ppermute | solution.py:12
  384.4 9.6 %collective-permute-start.4 = (bf16[4,64,64]{2,1,0:T(8,128)(2,1)S(1)}, bf16[4,64,64]{2,1,0:T(8,128)(2,1)S(1)}, u32[]{:S(2)}, u32[]{:S(2)}) collective-permute-start(bf16[4,64,64]{2,1,0:T(8,128)(2,1)S(1)} %copy.38), channel_id=1, source_target_pairs={{64,0},{128,64},{192,128},{256,192},{320,256},{384,320},{448,384},... | collective-permute-start | bytes 98312 | tf_op jit(solution)/shard_map/while/body/eval_jaxpr/ppermute | solution.py:12
  403.8 4.3 collective-permute-start.1
  410.6 7.4 %collective-permute-start.2 = (bf16[4,64,64]{2,1,0:T(8,128)(2,1)S(1)}, bf16[4,64,64]{2,1,0:T(8,128)(2,1)S(1)}, u32[]{:S(2)}, u32[]{:S(2)}) collective-permute-start(bf16[4,64,64]{2,1,0:T(8,128)(2,1)S(1)} %copy.36), channel_id=1, source_target_pairs={{64,0},{128,64},{192,128},{256,192},{320,256},{384,320},{448,384},... | collective-permute-start | bytes 98312 | tf_op jit(solution)/shard_map/while/body/eval_jaxpr/ppermute | solution.py:12
  418.0 9.6 %collective-permute-start.4 = (bf16[4,64,64]{2,1,0:T(8,128)(2,1)S(1)}, bf16[4,64,64]{2,1,0:T(8,128)(2,1)S(1)}, u32[]{:S(2)}, u32[]{:S(2)}) collective-permute-start(bf16[4,64,64]{2,1,0:T(8,128)(2,1)S(1)} %copy.38), channel_id=1, source_target_pairs={{64,0},{128,64},{192,128},{256,192},{320,256},{384,320},{448,384},... | collective-permute-start | bytes 98312 | tf_op jit(solution)/shard_map/while/body/eval_jaxpr/ppermute | solution.py:12
  441.8 7.4 %collective-permute-start.2 = (bf16[4,64,64]{2,1,0:T(8,128)(2,1)S(1)}, bf16[4,64,64]{2,1,0:T(8,128)(2,1)S(1)}, u32[]{:S(2)}, u32[]{:S(2)}) collective-permute-start(bf16[4,64,64]{2,1,0:T(8,128)(2,1)S(1)} %copy.36), channel_id=1, source_target_pairs={{64,0},{128,64},{192,128},{256,192},{320,256},{384,320},{448,384},... | collective-permute-start | bytes 98312 | tf_op jit(solution)/shard_map/while/body/eval_jaxpr/ppermute | solution.py:12
  449.2 9.6 %collective-permute-start.4 = (bf16[4,64,64]{2,1,0:T(8,128)(2,1)S(1)}, bf16[4,64,64]{2,1,0:T(8,128)(2,1)S(1)}, u32[]{:S(2)}, u32[]{:S(2)}) collective-permute-start(bf16[4,64,64]{2,1,0:T(8,128)(2,1)S(1)} %copy.38), channel_id=1, source_target_pairs={{64,0},{128,64},{192,128},{256,192},{320,256},{384,320},{448,384},... | collective-permute-start | bytes 98312 | tf_op jit(solution)/shard_map/while/body/eval_jaxpr/ppermute | solution.py:12
  468.6 4.3 collective-permute-start.1
  475.4 7.4 %collective-permute-start.2 = (bf16[4,64,64]{2,1,0:T(8,128)(2,1)S(1)}, bf16[4,64,64]{2,1,0:T(8,128)(2,1)S(1)}, u32[]{:S(2)}, u32[]{:S(2)}) collective-permute-start(bf16[4,64,64]{2,1,0:T(8,128)(2,1)S(1)} %copy.36), channel_id=1, source_target_pairs={{64,0},{128,64},{192,128},{256,192},{320,256},{384,320},{448,384},... | collective-permute-start | bytes 98312 | tf_op jit(solution)/shard_map/while/body/eval_jaxpr/ppermute | solution.py:12
  482.9 9.6 %collective-permute-start.4 = (bf16[4,64,64]{2,1,0:T(8,128)(2,1)S(1)}, bf16[4,64,64]{2,1,0:T(8,128)(2,1)S(1)}, u32[]{:S(2)}, u32[]{:S(2)}) collective-permute-start(bf16[4,64,64]{2,1,0:T(8,128)(2,1)S(1)} %copy.38), channel_id=1, source_target_pairs={{64,0},{128,64},{192,128},{256,192},{320,256},{384,320},{448,384},... | collective-permute-start | bytes 98312 | tf_op jit(solution)/shard_map/while/body/eval_jaxpr/ppermute | solution.py:12
  505.5 111.7 %reduce-scatter.2.cloned.1.call-done = f32[2,4,64,128]{3,2,0,1:T(8,128)} async-done(((f32[2,16,64,128]{3,2,0,1:T(8,128)}), f32[2,4,64,128]{3,2,0,1:T(8,128)}) %reduce-scatter.2.cloned.1.call-update) | async-done | bytes 262160 | tf_op jit(solution)/shard_map/reduce_scatter | solution.py:63
  (513 shorter events, 178.4 us)
Async XLA Ops:
  7.2 610.1 %reduce-scatter.2.cloned.1.call-start = ((), (), s32[]{:S(2)}) async-start(), calls=%async_computation.1 | async-start | bytes 1310720 | tf_op jit(solution)/shard_map/reduce_scatter | solution.py:63
  8.8 35.8 %collective-permute-start.1 = (s32[16,2]{1,0:T(8,128)S(1)}, s32[16,2]{1,0:T(8,128)S(1)}, u32[]{:S(2)}, u32[]{:S(2)}) collective-permute-start(s32[16,2]{1,0:T(8,128)S(1)} %copy.35), channel_id=1, source_target_pairs={{4,0},{8,4},{12,8},{16,12},{20,16},{24,20},{28,24},{32,28},{36,32}... | collective-permute-start | bytes 392 | tf_op jit(solution)/shard_map/while/body/eval_jaxpr/ppermute | solution.py:12
  16.4 28.1 %collective-permute-start = (bf16[16,64,128]{2,1,0:T(8,128)(2,1)S(1)}, bf16[16,64,128]{2,1,0:T(8,128)(2,1)S(1)}, u32[]{:S(2)}, u32[]{:S(2)}) collective-permute-start(bf16[16,64,128]{2,1,0:T(8,128)(2,1)S(1)} %copy.34), channel_id=1, source_target_pairs={{4,0},{8,4},{12,8},{16,12},{20,16},{24,20},{28,24},{32,28},{36,32}... | collective-permute-start | bytes 786440 | tf_op jit(solution)/shard_map/while/body/eval_jaxpr/ppermute | solution.py:12
  18.9 25.6 %collective-permute-start.2 = (bf16[4,64,64]{2,1,0:T(8,128)(2,1)S(1)}, bf16[4,64,64]{2,1,0:T(8,128)(2,1)S(1)}, u32[]{:S(2)}, u32[]{:S(2)}) collective-permute-start(bf16[4,64,64]{2,1,0:T(8,128)(2,1)S(1)} %copy.36), channel_id=1, source_target_pairs={{64,0},{128,64},{192,128},{256,192},{320,256},{384,320},{448,384},... | collective-permute-start | bytes 98312 | tf_op jit(solution)/shard_map/while/body/eval_jaxpr/ppermute | solution.py:12
  44.6 31.7 %collective-permute-start.1 = (s32[16,2]{1,0:T(8,128)S(1)}, s32[16,2]{1,0:T(8,128)S(1)}, u32[]{:S(2)}, u32[]{:S(2)}) collective-permute-start(s32[16,2]{1,0:T(8,128)S(1)} %copy.35), channel_id=1, source_target_pairs={{4,0},{8,4},{12,8},{16,12},{20,16},{24,20},{28,24},{32,28},{36,32}... | collective-permute-start | bytes 392 | tf_op jit(solution)/shard_map/while/body/eval_jaxpr/ppermute | solution.py:12
  46.8 29.6 %collective-permute-start = (bf16[16,64,128]{2,1,0:T(8,128)(2,1)S(1)}, bf16[16,64,128]{2,1,0:T(8,128)(2,1)S(1)}, u32[]{:S(2)}, u32[]{:S(2)}) collective-permute-start(bf16[16,64,128]{2,1,0:T(8,128)(2,1)S(1)} %copy.34), channel_id=1, source_target_pairs={{4,0},{8,4},{12,8},{16,12},{20,16},{24,20},{28,24},{32,28},{36,32}... | collective-permute-start | bytes 786440 | tf_op jit(solution)/shard_map/while/body/eval_jaxpr/ppermute | solution.py:12
  49.0 27.4 %collective-permute-start.2 = (bf16[4,64,64]{2,1,0:T(8,128)(2,1)S(1)}, bf16[4,64,64]{2,1,0:T(8,128)(2,1)S(1)}, u32[]{:S(2)}, u32[]{:S(2)}) collective-permute-start(bf16[4,64,64]{2,1,0:T(8,128)(2,1)S(1)} %copy.36), channel_id=1, source_target_pairs={{64,0},{128,64},{192,128},{256,192},{320,256},{384,320},{448,384},... | collective-permute-start | bytes 98312 | tf_op jit(solution)/shard_map/while/body/eval_jaxpr/ppermute | solution.py:12
  57.0 19.4 %collective-permute-start.4 = (bf16[4,64,64]{2,1,0:T(8,128)(2,1)S(1)}, bf16[4,64,64]{2,1,0:T(8,128)(2,1)S(1)}, u32[]{:S(2)}, u32[]{:S(2)}) collective-permute-start(bf16[4,64,64]{2,1,0:T(8,128)(2,1)S(1)} %copy.38), channel_id=1, source_target_pairs={{64,0},{128,64},{192,128},{256,192},{320,256},{384,320},{448,384},... | collective-permute-start | bytes 98312 | tf_op jit(solution)/shard_map/while/body/eval_jaxpr/ppermute | solution.py:12
  76.4 33.9 %collective-permute-start.1 = (s32[16,2]{1,0:T(8,128)S(1)}, s32[16,2]{1,0:T(8,128)S(1)}, u32[]{:S(2)}, u32[]{:S(2)}) collective-permute-start(s32[16,2]{1,0:T(8,128)S(1)} %copy.35), channel_id=1, source_target_pairs={{4,0},{8,4},{12,8},{16,12},{20,16},{24,20},{28,24},{32,28},{36,32}... | collective-permute-start | bytes 392 | tf_op jit(solution)/shard_map/while/body/eval_jaxpr/ppermute | solution.py:12
  81.0 29.3 %collective-permute-start = (bf16[16,64,128]{2,1,0:T(8,128)(2,1)S(1)}, bf16[16,64,128]{2,1,0:T(8,128)(2,1)S(1)}, u32[]{:S(2)}, u32[]{:S(2)}) collective-permute-start(bf16[16,64,128]{2,1,0:T(8,128)(2,1)S(1)} %copy.34), channel_id=1, source_target_pairs={{4,0},{8,4},{12,8},{16,12},{20,16},{24,20},{28,24},{32,28},{36,32}... | collective-permute-start | bytes 786440 | tf_op jit(solution)/shard_map/while/body/eval_jaxpr/ppermute | solution.py:12
  83.4 26.8 %collective-permute-start.2 = (bf16[4,64,64]{2,1,0:T(8,128)(2,1)S(1)}, bf16[4,64,64]{2,1,0:T(8,128)(2,1)S(1)}, u32[]{:S(2)}, u32[]{:S(2)}) collective-permute-start(bf16[4,64,64]{2,1,0:T(8,128)(2,1)S(1)} %copy.36), channel_id=1, source_target_pairs={{64,0},{128,64},{192,128},{256,192},{320,256},{384,320},{448,384},... | collective-permute-start | bytes 98312 | tf_op jit(solution)/shard_map/while/body/eval_jaxpr/ppermute | solution.py:12
  90.9 19.4 %collective-permute-start.4 = (bf16[4,64,64]{2,1,0:T(8,128)(2,1)S(1)}, bf16[4,64,64]{2,1,0:T(8,128)(2,1)S(1)}, u32[]{:S(2)}, u32[]{:S(2)}) collective-permute-start(bf16[4,64,64]{2,1,0:T(8,128)(2,1)S(1)} %copy.38), channel_id=1, source_target_pairs={{64,0},{128,64},{192,128},{256,192},{320,256},{384,320},{448,384},... | collective-permute-start | bytes 98312 | tf_op jit(solution)/shard_map/while/body/eval_jaxpr/ppermute | solution.py:12
  110.3 31.2 %collective-permute-start.1 = (s32[16,2]{1,0:T(8,128)S(1)}, s32[16,2]{1,0:T(8,128)S(1)}, u32[]{:S(2)}, u32[]{:S(2)}) collective-permute-start(s32[16,2]{1,0:T(8,128)S(1)} %copy.35), channel_id=1, source_target_pairs={{4,0},{8,4},{12,8},{16,12},{20,16},{24,20},{28,24},{32,28},{36,32}... | collective-permute-start | bytes 392 | tf_op jit(solution)/shard_map/while/body/eval_jaxpr/ppermute | solution.py:12
  112.5 29.0 %collective-permute-start = (bf16[16,64,128]{2,1,0:T(8,128)(2,1)S(1)}, bf16[16,64,128]{2,1,0:T(8,128)(2,1)S(1)}, u32[]{:S(2)}, u32[]{:S(2)}) collective-permute-start(bf16[16,64,128]{2,1,0:T(8,128)(2,1)S(1)} %copy.34), channel_id=1, source_target_pairs={{4,0},{8,4},{12,8},{16,12},{20,16},{24,20},{28,24},{32,28},{36,32}... | collective-permute-start | bytes 786440 | tf_op jit(solution)/shard_map/while/body/eval_jaxpr/ppermute | solution.py:12
  114.7 26.8 %collective-permute-start.2 = (bf16[4,64,64]{2,1,0:T(8,128)(2,1)S(1)}, bf16[4,64,64]{2,1,0:T(8,128)(2,1)S(1)}, u32[]{:S(2)}, u32[]{:S(2)}) collective-permute-start(bf16[4,64,64]{2,1,0:T(8,128)(2,1)S(1)} %copy.36), channel_id=1, source_target_pairs={{64,0},{128,64},{192,128},{256,192},{320,256},{384,320},{448,384},... | collective-permute-start | bytes 98312 | tf_op jit(solution)/shard_map/while/body/eval_jaxpr/ppermute | solution.py:12
  141.5 33.6 %collective-permute-start.1 = (s32[16,2]{1,0:T(8,128)S(1)}, s32[16,2]{1,0:T(8,128)S(1)}, u32[]{:S(2)}, u32[]{:S(2)}) collective-permute-start(s32[16,2]{1,0:T(8,128)S(1)} %copy.35), channel_id=1, source_target_pairs={{4,0},{8,4},{12,8},{16,12},{20,16},{24,20},{28,24},{32,28},{36,32}... | collective-permute-start | bytes 392 | tf_op jit(solution)/shard_map/while/body/eval_jaxpr/ppermute | solution.py:12
  145.8 29.3 %collective-permute-start = (bf16[16,64,128]{2,1,0:T(8,128)(2,1)S(1)}, bf16[16,64,128]{2,1,0:T(8,128)(2,1)S(1)}, u32[]{:S(2)}, u32[]{:S(2)}) collective-permute-start(bf16[16,64,128]{2,1,0:T(8,128)(2,1)S(1)} %copy.34), channel_id=1, source_target_pairs={{4,0},{8,4},{12,8},{16,12},{20,16},{24,20},{28,24},{32,28},{36,32}... | collective-permute-start | bytes 786440 | tf_op jit(solution)/shard_map/while/body/eval_jaxpr/ppermute | solution.py:12
  148.3 26.8 %collective-permute-start.2 = (bf16[4,64,64]{2,1,0:T(8,128)(2,1)S(1)}, bf16[4,64,64]{2,1,0:T(8,128)(2,1)S(1)}, u32[]{:S(2)}, u32[]{:S(2)}) collective-permute-start(bf16[4,64,64]{2,1,0:T(8,128)(2,1)S(1)} %copy.36), channel_id=1, source_target_pairs={{64,0},{128,64},{192,128},{256,192},{320,256},{384,320},{448,384},... | collective-permute-start | bytes 98312 | tf_op jit(solution)/shard_map/while/body/eval_jaxpr/ppermute | solution.py:12
  175.1 31.2 %collective-permute-start.1 = (s32[16,2]{1,0:T(8,128)S(1)}, s32[16,2]{1,0:T(8,128)S(1)}, u32[]{:S(2)}, u32[]{:S(2)}) collective-permute-start(s32[16,2]{1,0:T(8,128)S(1)} %copy.35), channel_id=1, source_target_pairs={{4,0},{8,4},{12,8},{16,12},{20,16},{24,20},{28,24},{32,28},{36,32}... | collective-permute-start | bytes 392 | tf_op jit(solution)/shard_map/while/body/eval_jaxpr/ppermute | solution.py:12
  177.3 29.0 %collective-permute-start = (bf16[16,64,128]{2,1,0:T(8,128)(2,1)S(1)}, bf16[16,64,128]{2,1,0:T(8,128)(2,1)S(1)}, u32[]{:S(2)}, u32[]{:S(2)}) collective-permute-start(bf16[16,64,128]{2,1,0:T(8,128)(2,1)S(1)} %copy.34), channel_id=1, source_target_pairs={{4,0},{8,4},{12,8},{16,12},{20,16},{24,20},{28,24},{32,28},{36,32}... | collective-permute-start | bytes 786440 | tf_op jit(solution)/shard_map/while/body/eval_jaxpr/ppermute | solution.py:12
  179.5 26.8 %collective-permute-start.2 = (bf16[4,64,64]{2,1,0:T(8,128)(2,1)S(1)}, bf16[4,64,64]{2,1,0:T(8,128)(2,1)S(1)}, u32[]{:S(2)}, u32[]{:S(2)}) collective-permute-start(bf16[4,64,64]{2,1,0:T(8,128)(2,1)S(1)} %copy.36), channel_id=1, source_target_pairs={{64,0},{128,64},{192,128},{256,192},{320,256},{384,320},{448,384},... | collective-permute-start | bytes 98312 | tf_op jit(solution)/shard_map/while/body/eval_jaxpr/ppermute | solution.py:12
  206.4 33.6 %collective-permute-start.1 = (s32[16,2]{1,0:T(8,128)S(1)}, s32[16,2]{1,0:T(8,128)S(1)}, u32[]{:S(2)}, u32[]{:S(2)}) collective-permute-start(s32[16,2]{1,0:T(8,128)S(1)} %copy.35), channel_id=1, source_target_pairs={{4,0},{8,4},{12,8},{16,12},{20,16},{24,20},{28,24},{32,28},{36,32}... | collective-permute-start | bytes 392 | tf_op jit(solution)/shard_map/while/body/eval_jaxpr/ppermute | solution.py:12
  210.7 29.3 %collective-permute-start = (bf16[16,64,128]{2,1,0:T(8,128)(2,1)S(1)}, bf16[16,64,128]{2,1,0:T(8,128)(2,1)S(1)}, u32[]{:S(2)}, u32[]{:S(2)}) collective-permute-start(bf16[16,64,128]{2,1,0:T(8,128)(2,1)S(1)} %copy.34), channel_id=1, source_target_pairs={{4,0},{8,4},{12,8},{16,12},{20,16},{24,20},{28,24},{32,28},{36,32}... | collective-permute-start | bytes 786440 | tf_op jit(solution)/shard_map/while/body/eval_jaxpr/ppermute | solution.py:12
  213.1 26.8 %collective-permute-start.2 = (bf16[4,64,64]{2,1,0:T(8,128)(2,1)S(1)}, bf16[4,64,64]{2,1,0:T(8,128)(2,1)S(1)}, u32[]{:S(2)}, u32[]{:S(2)}) collective-permute-start(bf16[4,64,64]{2,1,0:T(8,128)(2,1)S(1)} %copy.36), channel_id=1, source_target_pairs={{64,0},{128,64},{192,128},{256,192},{320,256},{384,320},{448,384},... | collective-permute-start | bytes 98312 | tf_op jit(solution)/shard_map/while/body/eval_jaxpr/ppermute | solution.py:12
  240.0 32.5 %collective-permute-start.1 = (s32[16,2]{1,0:T(8,128)S(1)}, s32[16,2]{1,0:T(8,128)S(1)}, u32[]{:S(2)}, u32[]{:S(2)}) collective-permute-start(s32[16,2]{1,0:T(8,128)S(1)} %copy.35), channel_id=1, source_target_pairs={{4,0},{8,4},{12,8},{16,12},{20,16},{24,20},{28,24},{32,28},{36,32}... | collective-permute-start | bytes 392 | tf_op jit(solution)/shard_map/while/body/eval_jaxpr/ppermute | solution.py:12
  242.2 30.3 %collective-permute-start = (bf16[16,64,128]{2,1,0:T(8,128)(2,1)S(1)}, bf16[16,64,128]{2,1,0:T(8,128)(2,1)S(1)}, u32[]{:S(2)}, u32[]{:S(2)}) collective-permute-start(bf16[16,64,128]{2,1,0:T(8,128)(2,1)S(1)} %copy.34), channel_id=1, source_target_pairs={{4,0},{8,4},{12,8},{16,12},{20,16},{24,20},{28,24},{32,28},{36,32}... | collective-permute-start | bytes 786440 | tf_op jit(solution)/shard_map/while/body/eval_jaxpr/ppermute | solution.py:12
  245.7 26.8 %collective-permute-start.2 = (bf16[4,64,64]{2,1,0:T(8,128)(2,1)S(1)}, bf16[4,64,64]{2,1,0:T(8,128)(2,1)S(1)}, u32[]{:S(2)}, u32[]{:S(2)}) collective-permute-start(bf16[4,64,64]{2,1,0:T(8,128)(2,1)S(1)} %copy.36), channel_id=1, source_target_pairs={{64,0},{128,64},{192,128},{256,192},{320,256},{384,320},{448,384},... | collective-permute-start | bytes 98312 | tf_op jit(solution)/shard_map/while/body/eval_jaxpr/ppermute | solution.py:12
  272.5 34.8 %collective-permute-start.1 = (s32[16,2]{1,0:T(8,128)S(1)}, s32[16,2]{1,0:T(8,128)S(1)}, u32[]{:S(2)}, u32[]{:S(2)}) collective-permute-start(s32[16,2]{1,0:T(8,128)S(1)} %copy.35), channel_id=1, source_target_pairs={{4,0},{8,4},{12,8},{16,12},{20,16},{24,20},{28,24},{32,28},{36,32}... | collective-permute-start | bytes 392 | tf_op jit(solution)/shard_map/while/body/eval_jaxpr/ppermute | solution.py:12
  278.1 29.3 %collective-permute-start = (bf16[16,64,128]{2,1,0:T(8,128)(2,1)S(1)}, bf16[16,64,128]{2,1,0:T(8,128)(2,1)S(1)}, u32[]{:S(2)}, u32[]{:S(2)}) collective-permute-start(bf16[16,64,128]{2,1,0:T(8,128)(2,1)S(1)} %copy.34), channel_id=1, source_target_pairs={{4,0},{8,4},{12,8},{16,12},{20,16},{24,20},{28,24},{32,28},{36,32}... | collective-permute-start | bytes 786440 | tf_op jit(solution)/shard_map/while/body/eval_jaxpr/ppermute | solution.py:12
  280.6 26.8 %collective-permute-start.2 = (bf16[4,64,64]{2,1,0:T(8,128)(2,1)S(1)}, bf16[4,64,64]{2,1,0:T(8,128)(2,1)S(1)}, u32[]{:S(2)}, u32[]{:S(2)}) collective-permute-start(bf16[4,64,64]{2,1,0:T(8,128)(2,1)S(1)} %copy.36), channel_id=1, source_target_pairs={{64,0},{128,64},{192,128},{256,192},{320,256},{384,320},{448,384},... | collective-permute-start | bytes 98312 | tf_op jit(solution)/shard_map/while/body/eval_jaxpr/ppermute | solution.py:12
  307.4 31.2 %collective-permute-start.1 = (s32[16,2]{1,0:T(8,128)S(1)}, s32[16,2]{1,0:T(8,128)S(1)}, u32[]{:S(2)}, u32[]{:S(2)}) collective-permute-start(s32[16,2]{1,0:T(8,128)S(1)} %copy.35), channel_id=1, source_target_pairs={{4,0},{8,4},{12,8},{16,12},{20,16},{24,20},{28,24},{32,28},{36,32}... | collective-permute-start | bytes 392 | tf_op jit(solution)/shard_map/while/body/eval_jaxpr/ppermute | solution.py:12
  309.6 29.0 %collective-permute-start = (bf16[16,64,128]{2,1,0:T(8,128)(2,1)S(1)}, bf16[16,64,128]{2,1,0:T(8,128)(2,1)S(1)}, u32[]{:S(2)}, u32[]{:S(2)}) collective-permute-start(bf16[16,64,128]{2,1,0:T(8,128)(2,1)S(1)} %copy.34), channel_id=1, source_target_pairs={{4,0},{8,4},{12,8},{16,12},{20,16},{24,20},{28,24},{32,28},{36,32}... | collective-permute-start | bytes 786440 | tf_op jit(solution)/shard_map/while/body/eval_jaxpr/ppermute | solution.py:12
  311.8 26.8 %collective-permute-start.2 = (bf16[4,64,64]{2,1,0:T(8,128)(2,1)S(1)}, bf16[4,64,64]{2,1,0:T(8,128)(2,1)S(1)}, u32[]{:S(2)}, u32[]{:S(2)}) collective-permute-start(bf16[4,64,64]{2,1,0:T(8,128)(2,1)S(1)} %copy.36), channel_id=1, source_target_pairs={{64,0},{128,64},{192,128},{256,192},{320,256},{384,320},{448,384},... | collective-permute-start | bytes 98312 | tf_op jit(solution)/shard_map/while/body/eval_jaxpr/ppermute | solution.py:12
  338.6 33.9 %collective-permute-start.1 = (s32[16,2]{1,0:T(8,128)S(1)}, s32[16,2]{1,0:T(8,128)S(1)}, u32[]{:S(2)}, u32[]{:S(2)}) collective-permute-start(s32[16,2]{1,0:T(8,128)S(1)} %copy.35), channel_id=1, source_target_pairs={{4,0},{8,4},{12,8},{16,12},{20,16},{24,20},{28,24},{32,28},{36,32}... | collective-permute-start | bytes 392 | tf_op jit(solution)/shard_map/while/body/eval_jaxpr/ppermute | solution.py:12
  343.2 29.3 %collective-permute-start = (bf16[16,64,128]{2,1,0:T(8,128)(2,1)S(1)}, bf16[16,64,128]{2,1,0:T(8,128)(2,1)S(1)}, u32[]{:S(2)}, u32[]{:S(2)}) collective-permute-start(bf16[16,64,128]{2,1,0:T(8,128)(2,1)S(1)} %copy.34), channel_id=1, source_target_pairs={{4,0},{8,4},{12,8},{16,12},{20,16},{24,20},{28,24},{32,28},{36,32}... | collective-permute-start | bytes 786440 | tf_op jit(solution)/shard_map/while/body/eval_jaxpr/ppermute | solution.py:12
  345.7 26.8 %collective-permute-start.2 = (bf16[4,64,64]{2,1,0:T(8,128)(2,1)S(1)}, bf16[4,64,64]{2,1,0:T(8,128)(2,1)S(1)}, u32[]{:S(2)}, u32[]{:S(2)}) collective-permute-start(bf16[4,64,64]{2,1,0:T(8,128)(2,1)S(1)} %copy.36), channel_id=1, source_target_pairs={{64,0},{128,64},{192,128},{256,192},{320,256},{384,320},{448,384},... | collective-permute-start | bytes 98312 | tf_op jit(solution)/shard_map/while/body/eval_jaxpr/ppermute | solution.py:12
  372.6 31.2 %collective-permute-start.1 = (s32[16,2]{1,0:T(8,128)S(1)}, s32[16,2]{1,0:T(8,128)S(1)}, u32[]{:S(2)}, u32[]{:S(2)}) collective-permute-start(s32[16,2]{1,0:T(8,128)S(1)} %copy.35), channel_id=1, source_target_pairs={{4,0},{8,4},{12,8},{16,12},{20,16},{24,20},{28,24},{32,28},{36,32}... | collective-permute-start | bytes 392 | tf_op jit(solution)/shard_map/while/body/eval_jaxpr/ppermute | solution.py:12
  374.8 29.0 %collective-permute-start = (bf16[16,64,128]{2,1,0:T(8,128)(2,1)S(1)}, bf16[16,64,128]{2,1,0:T(8,128)(2,1)S(1)}, u32[]{:S(2)}, u32[]{:S(2)}) collective-permute-start(bf16[16,64,128]{2,1,0:T(8,128)(2,1)S(1)} %copy.34), channel_id=1, source_target_pairs={{4,0},{8,4},{12,8},{16,12},{20,16},{24,20},{28,24},{32,28},{36,32}... | collective-permute-start | bytes 786440 | tf_op jit(solution)/shard_map/while/body/eval_jaxpr/ppermute | solution.py:12
  376.9 26.8 %collective-permute-start.2 = (bf16[4,64,64]{2,1,0:T(8,128)(2,1)S(1)}, bf16[4,64,64]{2,1,0:T(8,128)(2,1)S(1)}, u32[]{:S(2)}, u32[]{:S(2)}) collective-permute-start(bf16[4,64,64]{2,1,0:T(8,128)(2,1)S(1)} %copy.36), channel_id=1, source_target_pairs={{64,0},{128,64},{192,128},{256,192},{320,256},{384,320},{448,384},... | collective-permute-start | bytes 98312 | tf_op jit(solution)/shard_map/while/body/eval_jaxpr/ppermute | solution.py:12
  403.8 33.6 %collective-permute-start.1 = (s32[16,2]{1,0:T(8,128)S(1)}, s32[16,2]{1,0:T(8,128)S(1)}, u32[]{:S(2)}, u32[]{:S(2)}) collective-permute-start(s32[16,2]{1,0:T(8,128)S(1)} %copy.35), channel_id=1, source_target_pairs={{4,0},{8,4},{12,8},{16,12},{20,16},{24,20},{28,24},{32,28},{36,32}... | collective-permute-start | bytes 392 | tf_op jit(solution)/shard_map/while/body/eval_jaxpr/ppermute | solution.py:12
  408.1 29.3 %collective-permute-start = (bf16[16,64,128]{2,1,0:T(8,128)(2,1)S(1)}, bf16[16,64,128]{2,1,0:T(8,128)(2,1)S(1)}, u32[]{:S(2)}, u32[]{:S(2)}) collective-permute-start(bf16[16,64,128]{2,1,0:T(8,128)(2,1)S(1)} %copy.34), channel_id=1, source_target_pairs={{4,0},{8,4},{12,8},{16,12},{20,16},{24,20},{28,24},{32,28},{36,32}... | collective-permute-start | bytes 786440 | tf_op jit(solution)/shard_map/while/body/eval_jaxpr/ppermute | solution.py:12
  410.6 26.8 %collective-permute-start.2 = (bf16[4,64,64]{2,1,0:T(8,128)(2,1)S(1)}, bf16[4,64,64]{2,1,0:T(8,128)(2,1)S(1)}, u32[]{:S(2)}, u32[]{:S(2)}) collective-permute-start(bf16[4,64,64]{2,1,0:T(8,128)(2,1)S(1)} %copy.36), channel_id=1, source_target_pairs={{64,0},{128,64},{192,128},{256,192},{320,256},{384,320},{448,384},... | collective-permute-start | bytes 98312 | tf_op jit(solution)/shard_map/while/body/eval_jaxpr/ppermute | solution.py:12
  437.4 31.2 %collective-permute-start.1 = (s32[16,2]{1,0:T(8,128)S(1)}, s32[16,2]{1,0:T(8,128)S(1)}, u32[]{:S(2)}, u32[]{:S(2)}) collective-permute-start(s32[16,2]{1,0:T(8,128)S(1)} %copy.35), channel_id=1, source_target_pairs={{4,0},{8,4},{12,8},{16,12},{20,16},{24,20},{28,24},{32,28},{36,32}... | collective-permute-start | bytes 392 | tf_op jit(solution)/shard_map/while/body/eval_jaxpr/ppermute | solution.py:12
  439.6 29.0 %collective-permute-start = (bf16[16,64,128]{2,1,0:T(8,128)(2,1)S(1)}, bf16[16,64,128]{2,1,0:T(8,128)(2,1)S(1)}, u32[]{:S(2)}, u32[]{:S(2)}) collective-permute-start(bf16[16,64,128]{2,1,0:T(8,128)(2,1)S(1)} %copy.34), channel_id=1, source_target_pairs={{4,0},{8,4},{12,8},{16,12},{20,16},{24,20},{28,24},{32,28},{36,32}... | collective-permute-start | bytes 786440 | tf_op jit(solution)/shard_map/while/body/eval_jaxpr/ppermute | solution.py:12
  441.8 26.8 %collective-permute-start.2 = (bf16[4,64,64]{2,1,0:T(8,128)(2,1)S(1)}, bf16[4,64,64]{2,1,0:T(8,128)(2,1)S(1)}, u32[]{:S(2)}, u32[]{:S(2)}) collective-permute-start(bf16[4,64,64]{2,1,0:T(8,128)(2,1)S(1)} %copy.36), channel_id=1, source_target_pairs={{64,0},{128,64},{192,128},{256,192},{320,256},{384,320},{448,384},... | collective-permute-start | bytes 98312 | tf_op jit(solution)/shard_map/while/body/eval_jaxpr/ppermute | solution.py:12
  468.6 33.6 %collective-permute-start.1 = (s32[16,2]{1,0:T(8,128)S(1)}, s32[16,2]{1,0:T(8,128)S(1)}, u32[]{:S(2)}, u32[]{:S(2)}) collective-permute-start(s32[16,2]{1,0:T(8,128)S(1)} %copy.35), channel_id=1, source_target_pairs={{4,0},{8,4},{12,8},{16,12},{20,16},{24,20},{28,24},{32,28},{36,32}... | collective-permute-start | bytes 392 | tf_op jit(solution)/shard_map/while/body/eval_jaxpr/ppermute | solution.py:12
  472.9 29.3 %collective-permute-start = (bf16[16,64,128]{2,1,0:T(8,128)(2,1)S(1)}, bf16[16,64,128]{2,1,0:T(8,128)(2,1)S(1)}, u32[]{:S(2)}, u32[]{:S(2)}) collective-permute-start(bf16[16,64,128]{2,1,0:T(8,128)(2,1)S(1)} %copy.34), channel_id=1, source_target_pairs={{4,0},{8,4},{12,8},{16,12},{20,16},{24,20},{28,24},{32,28},{36,32}... | collective-permute-start | bytes 786440 | tf_op jit(solution)/shard_map/while/body/eval_jaxpr/ppermute | solution.py:12
  475.4 26.8 %collective-permute-start.2 = (bf16[4,64,64]{2,1,0:T(8,128)(2,1)S(1)}, bf16[4,64,64]{2,1,0:T(8,128)(2,1)S(1)}, u32[]{:S(2)}, u32[]{:S(2)}) collective-permute-start(bf16[4,64,64]{2,1,0:T(8,128)(2,1)S(1)} %copy.36), channel_id=1, source_target_pairs={{64,0},{128,64},{192,128},{256,192},{320,256},{384,320},{448,384},... | collective-permute-start | bytes 98312 | tf_op jit(solution)/shard_map/while/body/eval_jaxpr/ppermute | solution.py:12
  (49 other events, 399.2 us)
Sparse Core Ops, SparseCore 0:
  505.6 111.5 reduce-scatter.1
where the time goes:
time: 635 us; the launch traced here: 626 us
  starting transfers between devices  404 us (64%)
  waiting for transfers between devices  164 us (26%)
  local copies, waits for them, and re-layouts  22 us (3%)
  between operations  14.2 us (2%)
  other arithmetic  10.9 us (2%)
  matrix products  7.52 us (1%)
    ppermute x90, starting transfers between devices, passed_along(): return lax.ppermute(block, axis, route)  404 us
    reduce_scatter x1, waiting for transfers between devices, local(): summed = lax.psum_scatter(totals, 'layer', scatter_dimension=1, tiled=True)  112 us
    ppermute x90, waiting for transfers between devices, passed_along(): return lax.ppermute(block, axis, route)  52.1 us
  transfers between devices with their start and end apart: 91, of which 30 were waited for; matrix products, arithmetic and copies ran while one was open for 5% of the time, Pallas kernels for 0%

commit v1 on v0

v1 whole, which is shorter than its diff:
```python
import functools

import jax
import jax.numpy as jnp
from jax import lax
from jax.experimental import pallas as pl
from jax.experimental.pallas import tpu as pltpu
from jax.sharding import PartitionSpec as P

MESH = pl.DeviceIdType.MESH
BLK = 64
KB = 4
CB = 2
NX = 4
NY = 4
HEAD = 16
BODY = 4 * BLK
MSG = HEAD + BODY
CUT = HEAD + 2 * BLK
LANES = 2 * BLK


def swap_halves(x):
    return jnp.concatenate([x[:, BLK:], x[:, :BLK]], axis=1)


def kernel(
    n_row,
    n_layer,
    dens_ref,
    dids_ref,
    ham_ref,
    hids_ref,
    ovl_ref,
    oids_ref,
    outh_ref,
    outo_ref,
    amsg,
    abuf,
    bbuf,
    acc,
    send_sem,
    give_sem,
    first_sem,
    second_sem,
    ring_sem,
    pair_sem,
):
    n_col = NX * NY
    n_lo = n_row // 2
    n_z = n_lo * n_layer
    row, col, layer = lax.axis_index("row"), lax.axis_index("col"), lax.axis_index("layer")
    core = lax.rem(row, 2)
    z = layer * n_lo + row // 2
    x, y = lax.rem(col, NX), col // NX

    def at_z(other):
        return {"row": lax.rem(other, n_lo) * 2 + core, "col": col, "layer": other // n_lo}

    def at_xy(ox, oy):
        return {"row": row, "col": oy * NX + ox, "layer": layer}

    def at_layer(other):
        return {"row": row, "col": col, "layer": other}

    up, down = lax.rem(z + 1, n_z), lax.rem(z + n_z - 1, n_z)
    sibling = {"row": row + 1 - 2 * core, "col": col, "layer": layer}
    partners = [at_z(up), at_z(down), sibling]
    partners += [at_layer(lax.rem(layer + o, n_layer)) for o in range(1, n_layer)]
    partners += [at_xy(lax.rem(x + o, NX), y) for o in range(1, NX)]
    partners += [at_xy(x, lax.rem(y + o, NY)) for o in range(1, NY)]

    barrier = pltpu.get_barrier_semaphore()
    for partner in partners:
        pl.semaphore_signal(barrier, inc=1, device_id=partner, device_id_type=MESH)

    first_half = lax.broadcasted_iota(jnp.int32, (1, LANES), 1) < BLK
    pad = jnp.zeros((HEAD - 4, LANES), jnp.float32)

    def head(left, right):
        ids = jnp.where(first_half, left, right).astype(jnp.float32)
        return jnp.concatenate([ids, pad], axis=0).astype(jnp.bfloat16)

    dids = dids_ref[...]
    for q in range(n_layer):
        amsg[q, 0:HEAD, :] = head(dids[4 * q : 4 * q + 4, 0:1], dids[4 * q : 4 * q + 4, 1:2])
        amsg[q, HEAD:MSG, :] = dens_ref[4 * q : 4 * q + 4].reshape(BODY, LANES)
    abuf[layer, col] = amsg[layer]
    mine = z * 2 + core
    bbuf[mine, 0:HEAD, :] = head(hids_ref[...], oids_ref[...])
    bbuf[mine, HEAD:MSG, :] = jnp.concatenate(
        [ham_ref[...].reshape(BODY, BLK), ovl_ref[...].reshape(BODY, BLK)], axis=1
    )

    pl.semaphore_wait(barrier, len(partners))

    def copy(src, dst, sem, device):
        return pltpu.make_async_remote_copy(
            src_ref=src, dst_ref=dst, send_sem=send_sem, recv_sem=sem, device_id=device, device_id_type=MESH
        )

    sent = []

    def send(src, dst, sem, device):
        copy(src, dst, sem, device).start()
        sent.append((src, device))

    def received(ref, sem):
        copy(ref, ref, sem, sibling).wait_recv()

    halves = (pl.ds(0, CUT), pl.ds(CUT, MSG - CUT))

    def give_pieces():
        for o in range(1, n_layer):
            other = lax.rem(layer + o, n_layer)
            send(amsg.at[other], abuf.at[layer, col], give_sem.at[o], at_layer(other))

    def spread_x(l, j, half, sem):
        for o in range(1, NX):
            ref = abuf.at[l, j, halves[half]]
            send(ref, ref, sem(o), at_xy(lax.rem(x + o, NX), y))

    def spread_y(l, j, half, sem):
        for o in range(1, NY):
            ref = abuf.at[l, j, halves[half]]
            send(ref, ref, sem(o), at_xy(x, lax.rem(y + o, NY)))

    def first_phase(l, o):
        spread_x(l, col, 0, lambda k: first_sem.at[o, 0, k])
        spread_y(l, col, 1, lambda k: first_sem.at[o, 1, k])
        spread_y(l, col, 0, lambda k: second_sem.at[o, 0])
        spread_x(l, col, 1, lambda k: second_sem.at[o, 1])

    def second_phase(l, o):
        for k in range(1, max(NX, NY)):
            if k < NX:
                j = y * NX + lax.rem(x + NX - k, NX)
                received(abuf.at[l, j, halves[0]], first_sem.at[o, 0, k])
                spread_y(l, j, 0, lambda _: second_sem.at[o, 0])
            if k < NY:
                j = lax.rem(y + NY - k, NY) * NX + x
                received(abuf.at[l, j, halves[1]], first_sem.at[o, 1, k])
                spread_x(l, j, 1, lambda _: second_sem.at[o, 1])

    def gathered(l, o):
        received(abuf.at[l, pl.ds(0, NX * (NY - 1)), halves[0]], second_sem.at[o, 0])
        received(abuf.at[l, pl.ds(0, NY * (NX - 1)), halves[1]], second_sem.at[o, 1])

    def tile_of(plane):
        return lax.rem(plane + n_z, n_z) * 2 + core

    n_up, n_down = n_z // 2, n_z // 2 - 1

    def forward(s, way):
        ref = bbuf.at[tile_of(z - s if way == 0 else z + s)]
        send(ref, ref, ring_sem.at[way, s], at_z(up if way == 0 else down))

    def share(s, way):
        ref = bbuf.at[tile_of(z - s if way == 0 else z + s)]
        send(ref, ref, pair_sem.at[0], sibling)

    def arrived(s, way):
        ref = bbuf.at[tile_of(z - 1 - s if way == 0 else z + 1 + s)]
        received(ref, ring_sem.at[way, s])

    events = {}

    def other_layer(o):
        return lax.rem(layer + n_layer - o, n_layer)

    def take_piece(o):
        received(abuf.at[other_layer(o), col], give_sem.at[o])
        first_phase(other_layer(o), o)

    last = n_up - 1
    events.setdefault(min(1, last), []).append(lambda: second_phase(layer, 0))
    events.setdefault(min(5, last), []).append(lambda: (take_piece(1), take_piece(3)))
    events.setdefault(min(7, last), []).append(
        lambda: (second_phase(other_layer(1), 1), second_phase(other_layer(3), 3))
    )
    events.setdefault(min(10, last), []).append(lambda: take_piece(2))
    events.setdefault(min(12, last), []).append(lambda: second_phase(other_layer(2), 2))

    forward(0, 0)
    forward(0, 1)
    first_phase(layer, 0)
    give_pieces()
    share(0, 0)
    for s in range(n_up):
        arrived(s, 0)
        if s + 1 < n_up:
            forward(s + 1, 0)
        if s < n_down:
            arrived(s, 1)
            if s + 1 < n_down:
                forward(s + 1, 1)
        share(s + 1, 0)
        if s < n_down:
            share(s + 1, 1)
        for event in events.get(s, ()):
            event()
    for o in range(n_layer):
        gathered(other_layer(o), o)
    received(bbuf.at[pl.ds(0, n_z)], pair_sem.at[0])

    ones = jnp.ones((1, LANES), jnp.float32)
    left = jnp.where(first_half, ones, 0.0)
    lane_half = 1.0 - left

    def dense_a(l, j):
        ids = abuf[l, j, 0:HEAD, :].astype(jnp.float32)
        flip = swap_halves(ids)
        rows = []
        for r in range(4):
            data = abuf[l, j, HEAD + BLK * r : HEAD + BLK * (r + 1), :]
            turned = swap_halves(data)
            parts = []
            for base in (0.0, 2.0):
                want = lane_half + base
                keep = jnp.where(ids[r : r + 1] == want, 1.0, 0.0).astype(jnp.bfloat16)
                take = jnp.where(flip[r : r + 1] == want, 1.0, 0.0).astype(jnp.bfloat16)
                parts.append(data * keep + turned * take)
            rows.append(jnp.concatenate(parts, axis=1))
        return jnp.concatenate(rows, axis=0)

    def dense_b(f):
        ids = bbuf[f, 0:HEAD, :].astype(jnp.float32)
        flip = swap_halves(ids)
        rows = []
        for r in range(4):
            data = bbuf[f, HEAD + BLK * r : HEAD + BLK * (r + 1), :]
            turned = swap_halves(data)
            own, opp = ids[r : r + 1], flip[r : r + 1]

            def mask(which, value, side):
                return (jnp.where(which == value, 1.0, 0.0) * side).astype(jnp.bfloat16)

            ham = data * mask(own, 0.0, left) + turned * mask(opp, 1.0, lane_half)
            ovl = turned * mask(opp, 0.0, left) + data * mask(own, 1.0, lane_half)
            rows.append(jnp.concatenate([ham, ovl], axis=1))
        return jnp.concatenate(rows, axis=0)

    acc[...] = jnp.zeros_like(acc)

    def step(j, carry):
        for l in range(n_layer):
            group = lax.rem(row + j, n_row)
            f = l * n_row + lax.rem(group + n_row - col, n_row)
            acc[...] += jnp.dot(dense_a(l, j), dense_b(f), preferred_element_type=jnp.float32)
        return carry

    lax.fori_loop(0, n_col, step, 0)
    outh_ref[...] = acc[:, :LANES].reshape(4, BLK, LANES)
    outo_ref[...] = acc[:, LANES:].reshape(4, BLK, LANES)

    for ref, device in sent:
        copy(ref, ref, give_sem.at[0], device).wait_send()


def solution(mesh):
    n_row, n_col, n_layer = mesh.shape["row"], mesh.shape["col"], mesh.shape["layer"]
    n_z = n_row // 2 * n_layer

    def local(dens_blocks, dens_ids, ham_blocks, ham_ids, ovl_blocks, ovl_ids):
        out = jax.ShapeDtypeStruct((4, BLK, LANES), jnp.float32)
        return pl.pallas_call(
            functools.partial(kernel, n_row, n_layer),
            out_shape=(out, out),
            in_specs=[pl.BlockSpec(memory_space=pltpu.VMEM)] * 6,
            out_specs=[pl.BlockSpec(memory_space=pltpu.VMEM)] * 2,
            scratch_shapes=[
                pltpu.VMEM((n_layer, MSG, LANES), jnp.bfloat16),
                pltpu.VMEM((n_layer, n_col, MSG, LANES), jnp.bfloat16),
                pltpu.VMEM((n_z * 2, MSG, LANES), jnp.bfloat16),
                pltpu.VMEM((BODY, 2 * LANES), jnp.float32),
                pltpu.SemaphoreType.DMA,
                pltpu.SemaphoreType.DMA((n_layer,)),
                pltpu.SemaphoreType.DMA((n_layer, 2, max(NX, NY))),
                pltpu.SemaphoreType.DMA((n_layer, 2)),
                pltpu.SemaphoreType.DMA((2, n_z // 2)),
                pltpu.SemaphoreType.DMA((1,)),
            ],
            compiler_params=pltpu.CompilerParams(
                collective_id=0, has_side_effects=True, vmem_limit_bytes=40 * 1024 * 1024
            ),
        )(
            dens_blocks.reshape(4 * n_layer, BLK, LANES),
            dens_ids.reshape(4 * n_layer, 2),
            ham_blocks.reshape(KB, BLK, BLK),
            ham_ids.reshape(KB, 1),
            ovl_blocks.reshape(KB, BLK, BLK),
            ovl_ids.reshape(KB, 1),
        )

    tile = P("row", "col", "layer", None, None, None)
    ids = P("row", "col", "layer", None, None)
    out = P(("row", "layer"), None, "col")
    return jax.shard_map(
        local,
        mesh=mesh,
        in_specs=(tile, ids, tile, ids, tile, ids),
        out_specs=(out, out),
        check_vma=False,
    )
```

time: 635 us -> 122 us (0.19); the launches traced: 626 us -> 122 us
  starting transfers between devices: 404 us -> 0 us
  waiting for transfers between devices: 164 us -> 0 us
  Pallas kernels: 0 us -> 115 us
  local copies, waits for them, and re-layouts: 22 us -> 6 us
  between operations: 14.2 us -> 0.65 us
  other arithmetic: 10.9 us -> 0 us
  matrix products: 7.52 us -> 0 us
    ppermute x90 -> x0, starting transfers between devices: 404 us -> none  [passed_along(): return lax.ppermute(block, axis, route)]
    pallas_call x0 -> x1, Pallas kernels: none -> 115 us  [local(): pl.pallas_call(functools.partial(kernel, n_row, n_layer), out_shape=(out,...]
    reduce_scatter x1 -> x0, waiting for transfers between devices: 112 us -> none  [local(): summed = lax.psum_scatter(totals, 'layer', scatter_dimension=1, tiled=True)]
    ppermute x90 -> x0, waiting for transfers between devices: 52.1 us -> none  [passed_along(): return lax.ppermute(block, axis, route)]
    gather x16 -> x0, local copies, waits for them, and re-layouts: 12 us -> none  [product(): selected = jnp.take(stacked, dens_index, axis=1)]
    dot_general x16 -> x0, matrix products: 7.52 us -> none  [product(): jnp.einsum('rxk,mrkw->mrxw', dens_tile, selected, preferred_element_type=...]
  transfers between devices with their start and end apart: 91 -> 0, of which waited for: 30 -> 0; matrix products, arithmetic and copies ran while one was open for 5% -> 0% of each run, Pallas kernels for 0% -> 0%
where the time goes in v1:
time: 122 us
  Pallas kernels  115 us (94%)
  local copies, waits for them, and re-layouts  6 us (5%)
    pallas_call x1, Pallas kernels, local(): pl.pallas_call(functools.partial(kernel, n_row, n_layer), out_shape=(out,...  115 us
    unnamed x14, local copies, waits for them, and re-layouts  5.74 us

profile of v1, /device:TPU:1, one launch (start us, length us, event | category | flops | bytes accessed | tf_op | source)
XLA Modules:
  0.0 121.9 jit_solution(10081736989303902025)
XLA Ops:
  0.6 0.0 copy-start.4
  0.6 0.6 copy-done.4
  1.3 0.0 copy-start.5
  1.3 0.1 copy.9.hids_ref
  1.4 0.6 copy-done.5
  1.9 0.0 copy-start.3
  1.9 0.1 copy.10.oids_ref
  2.0 0.6 copy-done.3
  2.6 0.1 copy.8.dids_ref
  2.7 0.0 copy-start
  2.7 0.9 copy-done
  3.7 0.0 copy-start.1
  3.7 0.8 copy-done.1
  4.5 0.0 copy-start.2
  4.5 0.8 copy-done.2
  5.3 115.2 %shard_map.77 = (f32[4,64,128]{2,1,0:T(8,128)S(1)}, f32[4,64,128]{2,1,0:T(8,128)S(1)}) custom-call(bf16[16,64,128]{2,1,0:T(8,128)(2,1)S(1)} %bitcast.6, s32[16,2]{1,0:T(8,128)S(1)} %copy.8.dids_ref, bf16[4,64,64]{2,1,0:T(8,128)(2,1)S(1)} %bitcast.7, s32[4,1]{1,0:T(4,128)S(1)} %copy.9.hids_ref, bf16[4,64,64]{2,1,0:T(8,128)(2,1)S(1)} %bitcast.8, ...), custom_call_target="tpu_custom_call" | custom-call | tf_op jit(solution)/shard_map/pallas_call | solution.py:266
  120.6 0.7 copy.13
  121.2 0.7 copy.14
Async XLA Ops:
  0.6 0.7 copy-start.4
  1.3 0.7 copy-start.5
  1.9 0.7 copy-start.3
  2.7 0.9 copy-start
  3.7 0.8 copy-start.1
  4.5 0.8 copy-start.2

commit v2 on v1

v2 whole, which is shorter than its diff:
```python
import functools

import jax
import jax.numpy as jnp
from jax import lax
from jax.experimental import pallas as pl
from jax.experimental.pallas import tpu as pltpu
from jax.sharding import PartitionSpec as P

MESH = pl.DeviceIdType.MESH
BLK = 64
KB = 4
CB = 2
NX = 4
NY = 4
HEAD = 16
BODY = 4 * BLK
MSG = HEAD + BODY
CUT = HEAD + 2 * BLK
LANES = 2 * BLK


MSG_CUTS = (0, CUT, MSG)
EVENTS = (
    (-1, "give", 1, 0),
    (-1, "give", 3, 0),
    (-1, "first", 0, 0),
    (-1, "first", 0, 1),
    (0, "give", 1, 1),
    (0, "give", 3, 1),
    (1, "give", 2, 0),
    (2, "give", 2, 1),
    (2, "second", 0, 0),
    (2, "second", 0, 1),
    (4, "take", 1, 0),
    (4, "take", 3, 0),
    (5, "take", 1, 1),
    (5, "take", 3, 1),
    (6, "second", 1, 0),
    (6, "second", 3, 0),
    (7, "second", 1, 1),
    (7, "second", 3, 1),
    (8, "take", 2, 0),
    (9, "take", 2, 1),
    (9, "gathered", 0, 0),
    (9, "gathered", 0, 1),
    (9, "gathered", 1, 0),
    (9, "gathered", 1, 1),
    (9, "gathered", 3, 0),
    (9, "gathered", 3, 1),
    (9, "mul", 1, 3),
    (10, "mul", 3, 4),
    (11, "second", 2, 0),
    (11, "mul", 4, 5),
    (12, "second", 2, 1),
    (12, "mul", 5, 7),
    (13, "mul", 7, 9),
    (14, "gathered", 2, 0),
    (14, "gathered", 2, 1),
    (14, "mul", 9, 12),
    (15, "mul", 12, 15),
    (16, "mul", 15, 16),
)


def swap_halves(x):
    return pltpu.roll(x, BLK, 1)


def kernel(
    n_row,
    n_layer,
    dens_ref,
    dids_ref,
    ham_ref,
    hids_ref,
    ovl_ref,
    oids_ref,
    outh_ref,
    outo_ref,
    amsg,
    abuf,
    bbuf,
    acc,
    dids,
    hids,
    oids,
    ham,
    ovl,
    load_sem,
    send_sem,
    give_sem,
    first_sem,
    second_sem,
    ring_sem,
    pair_sem,
):
    n_col = NX * NY
    n_lo = n_row // 2
    n_z = n_lo * n_layer
    reach = n_z // 2
    row, col, layer = lax.axis_index("row"), lax.axis_index("col"), lax.axis_index("layer")
    core = lax.rem(row, 2)
    z = layer * n_lo + row // 2
    x, y = lax.rem(col, NX), col // NX
    way = 1 - 2 * core
    mine, theirs = core, 1 - core

    loads = [
        pltpu.make_async_copy(dids_ref, dids, load_sem.at[0]),
        pltpu.make_async_copy(hids_ref, hids, load_sem.at[1]),
        pltpu.make_async_copy(oids_ref, oids, load_sem.at[2]),
        pltpu.make_async_copy(ham_ref, ham, load_sem.at[3]),
        pltpu.make_async_copy(ovl_ref, ovl, load_sem.at[4]),
    ]
    loads += [
        pltpu.make_async_copy(
            dens_ref.at[pl.ds(BODY * q, BODY)], amsg.at[q, pl.ds(HEAD, BODY)], load_sem.at[5 + q]
        )
        for q in range(n_layer)
    ]
    loads.append(
        pltpu.make_async_copy(
            dens_ref.at[pl.ds(BODY * layer, BODY)],
            abuf.at[layer, col, pl.ds(HEAD, BODY)],
            load_sem.at[5 + n_layer],
        )
    )
    for load in loads:
        load.start()

    def at_z(other):
        return {"row": lax.rem(other, n_lo) * 2 + core, "col": col, "layer": other // n_lo}

    def at_xy(ox, oy):
        return {"row": row, "col": oy * NX + ox, "layer": layer}

    def at_layer(other):
        return {"row": row, "col": col, "layer": other}

    onward = at_z(lax.rem(z + way + n_z, n_z))
    behind_z = lax.rem(z - way + n_z, n_z)
    behind = at_z(behind_z)
    sibling = {"row": row + 1 - 2 * core, "col": col, "layer": layer}
    across = {"row": lax.rem(behind_z, n_lo) * 2 + 1 - core, "col": col, "layer": behind_z // n_lo}
    partners = [onward, behind, across, sibling]
    partners += [at_layer(lax.rem(layer + o, n_layer)) for o in range(1, n_layer)]
    partners += [at_xy(lax.rem(x + o, NX), y) for o in range(1, NX)]
    partners += [at_xy(x, lax.rem(y + o, NY)) for o in range(1, NY)]

    barrier = pltpu.get_barrier_semaphore()
    for partner in partners:
        pl.semaphore_signal(barrier, inc=1, device_id=partner, device_id_type=MESH)

    first_half = lax.broadcasted_iota(jnp.int32, (1, LANES), 1) < BLK

    def head(left, right):
        n = left.shape[1]
        at_row = lax.broadcasted_iota(jnp.int32, (HEAD, n), 0)
        at_lane = lax.broadcasted_iota(jnp.int32, (HEAD, n), 1)
        turn = lambda ids: jnp.sum(jnp.where(at_row == at_lane, ids, 0.0), axis=1, keepdims=True)
        return jnp.where(first_half, turn(left), turn(right))

    for load in loads:
        load.wait()
    whole = head(dids[0:1, :].astype(jnp.float32), dids[1:2, :].astype(jnp.float32))
    pad = jnp.zeros((HEAD - 4, LANES), jnp.float32)
    for q in range(n_layer):
        piece = jnp.concatenate([whole[4 * q : 4 * q + 4], pad], axis=0)
        amsg[q, 0:HEAD, :] = piece.astype(jnp.bfloat16)
    abuf[layer, col, 0:HEAD, :] = amsg[layer, 0:HEAD, :]
    own_tile = z * 2 + core
    bbuf[own_tile, 0:HEAD, :] = head(
        hids[...].astype(jnp.float32), oids[...].astype(jnp.float32)
    ).astype(jnp.bfloat16)
    bbuf[own_tile, HEAD:MSG, :] = jnp.concatenate([ham[...], ovl[...]], axis=1)
    acc[...] = jnp.zeros_like(acc)

    pl.semaphore_wait(barrier, len(partners))

    def copy(src, dst, sem, device):
        return pltpu.make_async_remote_copy(
            src_ref=src, dst_ref=dst, send_sem=send_sem, recv_sem=sem, device_id=device, device_id_type=MESH
        )

    sent = []

    def send(src, dst, sem, device):
        copy(src, dst, sem, device).start()
        sent.append((src, device))

    def received(ref, sem):
        copy(ref, ref, sem, sibling).wait_recv()

    halves = (pl.ds(0, CUT), pl.ds(CUT, MSG - CUT))

    def other_layer(o):
        return lax.rem(layer + n_layer - o, n_layer)

    def give(o, half):
        other = lax.rem(layer + o, n_layer)
        send(
            amsg.at[other, halves[half]],
            abuf.at[layer, col, halves[half]],
            give_sem.at[o, half],
            at_layer(other),
        )

    def spread(o, j, half, along_x, sem):
        ref = abuf.at[other_layer(o), j, halves[half]]
        for k in range(1, NX if along_x else NY):
            where = at_xy(lax.rem(x + k, NX), y) if along_x else at_xy(x, lax.rem(y + k, NY))
            send(ref, ref, sem(k), where)

    def first_phase(o, half):
        spread(o, col, half, half == 0, lambda k: first_sem.at[o, half, k])
        spread(o, col, half, half == 1, lambda k: second_sem.at[o, half])

    def second_phase(o, half):
        for k in range(1, NX if half == 0 else NY):
            if half == 0:
                j = y * NX + lax.rem(x + NX - k, NX)
            else:
                j = lax.rem(y + NY - k, NY) * NX + x
            received(abuf.at[other_layer(o), j, halves[half]], first_sem.at[o, half, k])
            spread(o, j, half, half == 1, lambda _: second_sem.at[o, half])

    def gathered(o, half):
        n = NX * (NY - 1) if half == 0 else NY * (NX - 1)
        received(abuf.at[other_layer(o), pl.ds(0, n), halves[half]], second_sem.at[o, half])

    def take(o, half):
        received(abuf.at[other_layer(o), col, halves[half]], give_sem.at[o, half])
        first_phase(o, half)

    steps = {"give": give, "take": take, "first": first_phase, "second": second_phase, "gathered": gathered}

    parts = [pl.ds(MSG_CUTS[k], MSG_CUTS[k + 1] - MSG_CUTS[k]) for k in range(len(MSG_CUTS) - 1)]

    def tile(s, which, direction):
        return lax.rem(z - direction * s + n_z, n_z) * 2 + which

    def pass_on(s, which, k, w, device):
        ref = bbuf.at[tile(s, which, way), parts[k]]
        send(ref, ref, ring_sem.at[s, w, k], device)

    def share(s, which, w):
        ref = bbuf.at[tile(s, which, way)]
        send(ref, ref, pair_sem.at[s, w], sibling)

    def arrived(s, which, k, w):
        received(bbuf.at[tile(s + 1, which, way), parts[k]], ring_sem.at[s, w, k])

    def shared(s, which, w):
        received(bbuf.at[tile(s, which, -way)], pair_sem.at[s, w])

    n_parts = len(parts)

    left = jnp.where(first_half, jnp.ones((1, LANES), jnp.float32), 0.0)
    lane_half = 1.0 - left

    def dense_a(l, j):
        ids = abuf[l, j, 0:HEAD, :].astype(jnp.float32)
        flip = swap_halves(ids)
        rows = []
        for r in range(4):
            data = abuf[l, j, HEAD + BLK * r : HEAD + BLK * (r + 1), :]
            turned = swap_halves(data)
            parts = []
            for base in (0.0, 2.0):
                want = lane_half + base
                keep = jnp.where(ids[r : r + 1] == want, 1.0, 0.0).astype(jnp.bfloat16)
                take = jnp.where(flip[r : r + 1] == want, 1.0, 0.0).astype(jnp.bfloat16)
                parts.append(data * keep + turned * take)
            rows.append(jnp.concatenate(parts, axis=1))
        return jnp.concatenate(rows, axis=0)

    def dense_b(f):
        ids = bbuf[f, 0:HEAD, :].astype(jnp.float32)
        flip = swap_halves(ids)
        rows = []
        for r in range(4):
            data = bbuf[f, HEAD + BLK * r : HEAD + BLK * (r + 1), :]
            turned = swap_halves(data)
            own, opp = ids[r : r + 1], flip[r : r + 1]

            def mask(which, value, side):
                return (jnp.where(which == value, 1.0, 0.0) * side).astype(jnp.bfloat16)

            ham = data * mask(own, 0.0, left) + turned * mask(opp, 1.0, lane_half)
            ovl = turned * mask(opp, 0.0, left) + data * mask(own, 1.0, lane_half)
            rows.append(jnp.concatenate([ham, ovl], axis=1))
        return jnp.concatenate(rows, axis=0)

    def multiply(tiles):
        lhs, rhs = [], []
        for f in tiles:
            j = lax.rem(lax.rem(f, n_row) + col + n_row - row, n_row)
            lhs.append(dense_a(f // n_row, j))
            rhs.append(dense_b(f))
        acc[...] += jnp.dot(
            jnp.concatenate(lhs, axis=1), jnp.concatenate(rhs, axis=0), preferred_element_type=jnp.float32
        )

    def multiply_at(s, carry):
        for w in range(2):
            shared(s, w, w)
        multiply([tile(s, 0, 1), tile(s, 1, 1), tile(s, 0, -1), tile(s, 1, -1)])
        return carry

    events = {}
    for at, kind, o, half in EVENTS:
        events.setdefault(at if at < 0 else min(at, reach), []).append((kind, o, half))

    def run_events(at):
        for kind, o, half in events.get(at, ()):
            if kind == "mul":
                lax.fori_loop(o, min(half, reach), multiply_at, 0)
            else:
                steps[kind](o, half)

    for k in range(n_parts):
        ref = bbuf.at[own_tile, parts[k]]
        send(ref, ref, ring_sem.at[0, mine, k], onward)
        send(ref, ref, ring_sem.at[0, mine, k], across)
    share(0, mine, 0)
    run_events(-1)
    for s in range(reach):
        last = s == reach - 1
        for w in range(1 if last else 2):
            for k in range(n_parts):
                arrived(s, mine if last else w, k, w)
                if s + 2 < reach:
                    pass_on(s + 1, w, k, w, onward)
        if s + 2 == reach:
            for k in range(n_parts):
                pass_on(s + 1, mine, k, 0, onward)
        for w in range(1 if last else 2):
            share(s + 1, mine if last else w, w)
        run_events(s)
    run_events(reach)
    shared(0, theirs, 0)
    shared(reach, theirs, 0)
    multiply([tile(0, 0, 1), tile(0, 1, 1), tile(reach, 0, 1), tile(reach, 1, 1)])
    outh_ref[...] = acc[:, :LANES].reshape(4, BLK, LANES)
    outo_ref[...] = acc[:, LANES:].reshape(4, BLK, LANES)
    for ref, device in sent:
        copy(ref, ref, give_sem.at[0, 0], device).wait_send()


def solution(mesh):
    n_row, n_col, n_layer = mesh.shape["row"], mesh.shape["col"], mesh.shape["layer"]
    n_z = n_row // 2 * n_layer

    def local(dens_blocks, dens_ids, ham_blocks, ham_ids, ovl_blocks, ovl_ids):
        out = jax.ShapeDtypeStruct((4, BLK, LANES), jnp.float32)
        return pl.pallas_call(
            functools.partial(kernel, n_row, n_layer),
            out_shape=(out, out),
            in_specs=[pl.BlockSpec(memory_space=pltpu.HBM)] * 6,
            out_specs=[pl.BlockSpec(memory_space=pltpu.VMEM)] * 2,
            scratch_shapes=[
                pltpu.VMEM((n_layer, MSG, LANES), jnp.bfloat16),
                pltpu.VMEM((n_layer, n_col, MSG, LANES), jnp.bfloat16),
                pltpu.VMEM((n_z * 2, MSG, LANES), jnp.bfloat16),
                pltpu.VMEM((BODY, 2 * LANES), jnp.float32),
                pltpu.VMEM((2, 4 * n_layer), jnp.int32),
                pltpu.VMEM((1, KB), jnp.int32),
                pltpu.VMEM((1, KB), jnp.int32),
                pltpu.VMEM((BODY, BLK), jnp.bfloat16),
                pltpu.VMEM((BODY, BLK), jnp.bfloat16),
                pltpu.SemaphoreType.DMA((6 + n_layer,)),
                pltpu.SemaphoreType.DMA,
                pltpu.SemaphoreType.DMA((n_layer, 2)),
                pltpu.SemaphoreType.DMA((n_layer, 2, max(NX, NY))),
                pltpu.SemaphoreType.DMA((n_layer, 2)),
                pltpu.SemaphoreType.DMA((n_z // 2, 2, len(MSG_CUTS) - 1)),
                pltpu.SemaphoreType.DMA((n_z // 2 + 1, 2)),
            ],
            compiler_params=pltpu.CompilerParams(
                collective_id=0, has_side_effects=True, vmem_limit_bytes=60 * 1024 * 1024
            ),
        )(
            dens_blocks.reshape(4 * n_layer * BLK, LANES),
            dens_ids.reshape(4 * n_layer, 2).T,
            ham_blocks.reshape(KB * BLK, BLK),
            ham_ids.reshape(1, KB),
            ovl_blocks.reshape(KB * BLK, BLK),
            ovl_ids.reshape(1, KB),
        )

    tile = P("row", "col", "layer", None, None, None)
    ids = P("row", "col", "layer", None, None)
    out = P(("row", "layer"), None, "col")
    return jax.shard_map(
        local,
        mesh=mesh,
        in_specs=(tile, ids, tile, ids, tile, ids),
        out_specs=(out, out),
        check_vma=False,
    )
```

time: 122 us -> 102 us (0.84)
  Pallas kernels: 115 us -> 99.2 us
  local copies, waits for them, and re-layouts: 6 us -> 2.26 us
    pallas_call x1, Pallas kernels: 115 us -> 99.2 us  [local(): pl.pallas_call(functools.partial(kernel, n_row, n_layer), out_shape=(out,...]
    unnamed x14 -> x4, local copies, waits for them, and re-layouts: 5.74 us -> 2.26 us
where the time goes in v2:
time: 102 us
  Pallas kernels  99.2 us (97%)
  local copies, waits for them, and re-layouts  2.26 us (2%)
    pallas_call x1, Pallas kernels, local(): pl.pallas_call(functools.partial(kernel, n_row, n_layer), out_shape=(out,...  99.2 us
    unnamed x4, local copies, waits for them, and re-layouts  2.26 us

profile of v2, /device:TPU:1, one launch (start us, length us, event | category | flops | bytes accessed | tf_op | source)
XLA Modules:
  0.0 102.1 jit_solution(12502043230177448795)
XLA Ops:
  0.6 99.2 %shard_map.77 = (f32[4,64,128]{2,1,0:T(8,128)}, f32[4,64,128]{2,1,0:T(8,128)}) custom-call(bf16[1024,128]{1,0:T(8,128)(2,1)} %bitcast.8, s32[2,16]{1,0:T(2,128)} %bitcast.11, bf16[256,64]{1,0:T(8,128)(2,1)} %bitcast.9, s32[1,4]{1,0:T(1,128)} %bitcast.12, bf16[256,64]{1,0:T(8,128)(2,1)} %bitcast.10, s32[1,4]{1,0:T(1,128)} %bitcast.13), custom_call_target="tpu_custom_call" | custom-call | tf_op jit(solution)/shard_map/pallas_call | solution.py:357
  99.8 0.0 copy-start
  99.8 1.6 %copy.10 = f32[4,64,128]{2,1,0:T(8,128)} copy(f32[4,64,128]{2,1,0:T(8,128)} %get-tuple-element.4) | data formatting | bytes 262144
  101.4 0.0 copy-done
  101.4 0.7 copy.11
Async XLA Ops:
  99.8 1.6 %copy-start = (f32[4,64,128]{2,1,0:T(8,128)S(1)}, f32[4,64,128]{2,1,0:T(8,128)}, u32[]{:S(2)}) copy-start(f32[4,64,128]{2,1,0:T(8,128)} %get-tuple-element.5) | copy-start | bytes 393220

commit v3 on v2

--- a/solution.py
+++ b/solution.py
@@ -44,22 +44,21 @@
     (9, "take", 2, 1),
     (9, "gathered", 0, 0),
     (9, "gathered", 0, 1),
-    (9, "gathered", 1, 0),
-    (9, "gathered", 1, 1),
-    (9, "gathered", 3, 0),
-    (9, "gathered", 3, 1),
-    (9, "mul", 1, 3),
-    (10, "mul", 3, 4),
+    (10, "gathered", 1, 0),
+    (10, "gathered", 1, 1),
+    (10, "gathered", 3, 0),
+    (10, "gathered", 3, 1),
+    (10, "mul", 1, 3),
     (11, "second", 2, 0),
-    (11, "mul", 4, 5),
+    (11, "mul", 3, 4),
     (12, "second", 2, 1),
-    (12, "mul", 5, 7),
-    (13, "mul", 7, 9),
+    (12, "mul", 4, 6),
+    (13, "mul", 6, 9),
     (14, "gathered", 2, 0),
     (14, "gathered", 2, 1),
-    (14, "mul", 9, 12),
-    (15, "mul", 12, 15),
-    (16, "mul", 15, 16),
+    (14, "mul", 9, 11),
+    (15, "mul", 11, 13),
+    (16, "mul", 13, 16),
 )
 
 

time: 102 us -> 100 us (0.980)
  Pallas kernels: 99.2 us -> 96.9 us
    pallas_call x1, Pallas kernels: 99.2 us -> 96.9 us  [local(): pl.pallas_call(functools.partial(kernel, n_row, n_layer), out_shape=(out,...]
where the time goes in v3:
time: 100 us; the launch traced here: 99.8 us
  Pallas kernels  96.9 us (97%)
  local copies, waits for them, and re-layouts  2.26 us (2%)
    pallas_call x1, Pallas kernels, local(): pl.pallas_call(functools.partial(kernel, n_row, n_layer), out_shape=(out,...  96.9 us
    unnamed x4, local copies, waits for them, and re-layouts  2.26 us

profile of v3, /device:TPU:1, one launch (start us, length us, event | category | flops | bytes accessed | tf_op | source)
XLA Modules:
  0.0 99.8 jit_solution(12468965298767510460)
XLA Ops:
  0.6 96.9 %shard_map.77 = (f32[4,64,128]{2,1,0:T(8,128)}, f32[4,64,128]{2,1,0:T(8,128)}) custom-call(bf16[1024,128]{1,0:T(8,128)(2,1)} %bitcast.8, s32[2,16]{1,0:T(2,128)} %bitcast.11, bf16[256,64]{1,0:T(8,128)(2,1)} %bitcast.9, s32[1,4]{1,0:T(1,128)} %bitcast.12, bf16[256,64]{1,0:T(8,128)(2,1)} %bitcast.10, s32[1,4]{1,0:T(1,128)} %bitcast.13), custom_call_target="tpu_custom_call" | custom-call | tf_op jit(solution)/shard_map/pallas_call | solution.py:356
  97.5 0.0 copy-start
  97.5 1.6 %copy.10 = f32[4,64,128]{2,1,0:T(8,128)} copy(f32[4,64,128]{2,1,0:T(8,128)} %get-tuple-element.4) | data formatting | bytes 262144
  99.1 0.0 copy-done
  99.1 0.7 copy.11
Async XLA Ops:
  97.5 1.6 %copy-start = (f32[4,64,128]{2,1,0:T(8,128)S(1)}, f32[4,64,128]{2,1,0:T(8,128)}, u32[]{:S(2)}) copy-start(f32[4,64,128]{2,1,0:T(8,128)} %get-tuple-element.5) | copy-start | bytes 393220
